TPU v7x, 32 devices: a whole 2x2x4 slice. The times are simulated.
32 devices in a mesh: tok: 8 (over z, y), wid: 4 (over x, core).
Axes of the slice: x: 2, y: 2, z: 4, core: 2. Of those that a mesh axis runs over, the one named last changes fastest.
Arguments:
- queries: bfloat16 [1024, 8192], P('tok', 'wid'), may hold values from -6 to 6
- key_branch: bfloat16 [1024, 8192], P('tok', 'wid'), may hold values from -6 to 6
- value_branch: bfloat16 [1024, 8192], P('tok', 'wid'), may hold values from -6 to 6
- filters: float32 [512, 128], P('wid'), may hold values from -0.5 to 0.5
- out_weight: bfloat16 [8192, 8192], P(None, 'wid'), may hold values from -0.09375 to 0.09375
- cotangent: bfloat16 [1024, 8192], P('tok', 'wid'), may hold values from -6 to 6
Outputs:
- layer_out: bfloat16 [1024, 8192], P('tok', 'wid')
- grad_queries: bfloat16 [1024, 8192], P('tok', 'wid')
- grad_keys: bfloat16 [1024, 8192], P('tok', 'wid')
- grad_values: bfloat16 [1024, 8192], P('tok', 'wid')
- grad_filters: float32 [512, 128], P('wid')
All inputs are finite; a program needn't handle non-finite values.
Results may differ from a plain program's by a relative error of at most 0.02.
Values may be sent and summed in bfloat16 or wider, within the bound.
A program may use at most 192 MiB of HBM per device.

v0:
```python
import math

import jax
import jax.numpy as jnp
from jax import lax
from jax.sharding import PartitionSpec as P


def shifted(block, axis, distance):
    devices = range(lax.axis_size(axis))
    route = [(i - distance, i) for i in devices if i - distance in devices]
    return lax.ppermute(block, axis, route)


def causal_matrix(filters):
    groups, kernel = filters.shape
    span = 2 * kernel
    reverse = filters[:, ::-1]
    padded = jnp.concatenate(
        [
            jnp.zeros((groups, 1), jnp.float32),
            reverse,
            jnp.zeros((groups, span - kernel), jnp.float32),
        ],
        axis=1,
    )
    tiled = jnp.tile(padded, (1, kernel))[:, : kernel * span]
    return tiled.reshape(groups, kernel, span)


def split_pair(matrix):
    upper = matrix.astype(jnp.bfloat16)
    lower = (matrix - upper.astype(jnp.float32)).astype(jnp.bfloat16)
    return (upper, lower)


def split_einsum(form, pair, data):
    first = jnp.einsum(form, pair[0], data, preferred_element_type=jnp.float32)
    second = jnp.einsum(form, pair[1], data, preferred_element_type=jnp.float32)
    return first + second


def block_windows(extended, kernel, groups, group_size):
    blocks = extended.reshape(extended.shape[0] // kernel, kernel, groups, group_size)
    return jnp.concatenate([blocks[:-1], blocks[1:]], axis=1)


def gated_gradient(cotangent, out_weight):
    return (
        lax.psum_scatter(
            lax.dot_general(
                out_weight, cotangent, (((1,), (1,)), ((), ())), preferred_element_type=jnp.float32
            ).astype(jnp.bfloat16),
            "wid",
            scatter_dimension=0,
            tiled=True,
        )
        .astype(jnp.float32)
        .T
    )


def local(queries, key_branch, value_branch, filters, out_weight, cotangent):
    length, width = queries.shape
    groups, kernel = filters.shape
    group_size = width // groups
    nblocks = length // kernel
    kv = (key_branch.astype(jnp.float32) * value_branch.astype(jnp.float32)).astype(jnp.bfloat16)
    rim = shifted(kv, "tok", 1)
    extended = jnp.concatenate([rim, kv], axis=0)
    windows = block_windows(extended, kernel, groups, group_size)
    toeplitz = split_pair(causal_matrix(filters))
    conv = split_einsum("gts,bsgc->btgc", toeplitz, windows).reshape(length, width)
    gated = (queries.astype(jnp.float32) * conv).astype(jnp.bfloat16)
    layer_out = jnp.dot(
        lax.all_gather(gated, "wid", axis=1, tiled=True),
        out_weight,
        preferred_element_type=jnp.float32,
    ).astype(jnp.bfloat16)
    grad_gated = gated_gradient(cotangent, out_weight)
    grad_conv = (grad_gated * queries.astype(jnp.float32)).astype(jnp.bfloat16)
    grad_queries = (grad_gated * conv).astype(jnp.bfloat16)
    grad_blocks = grad_conv.reshape(nblocks, kernel, groups, group_size)
    spread = split_einsum("gts,btgc->bsgc", toeplitz, grad_blocks)
    lower_half = spread[:, :kernel]
    upper_half = spread[:, kernel:]
    returned = shifted(lower_half[0].reshape(kernel, width).astype(jnp.bfloat16), "tok", -1).astype(
        jnp.float32
    )
    tail = jnp.concatenate(
        [lower_half[1:], returned.reshape(1, kernel, groups, group_size)], axis=0
    )
    grad_kv = (upper_half + tail).reshape(length, width)
    grad_keys = (grad_kv * value_branch.astype(jnp.float32)).astype(jnp.bfloat16)
    grad_values = (grad_kv * key_branch.astype(jnp.float32)).astype(jnp.bfloat16)
    products = jnp.einsum(
        "btgc,bsgc->gts", grad_blocks, windows, preferred_element_type=jnp.float32
    )
    flat = jnp.pad(products.reshape(groups, kernel * 2 * kernel), ((0, 0), (0, kernel)))
    skewed = flat.reshape(groups, kernel, 2 * kernel + 1).sum(axis=1)
    local_terms = skewed[:, 1 : kernel + 1][:, ::-1]
    summed = lax.psum(local_terms, "tok")
    scale_factor = 1.0 / math.sqrt(length * lax.axis_size("tok") * group_size)
    grad_filters = summed * scale_factor
    return (layer_out, grad_queries, grad_keys, grad_values, grad_filters)


def solution(mesh):
    return jax.shard_map(
        local,
        mesh=mesh,
        in_specs=(
            P("tok", "wid"),
            P("tok", "wid"),
            P("tok", "wid"),
            P("wid", None),
            P(None, "wid"),
            P("tok", "wid"),
        ),
        out_specs=(
            P("tok", "wid"),
            P("tok", "wid"),
            P("tok", "wid"),
            P("tok", "wid"),
            P("wid", None),
        ),
        check_vma=False,
    )
```

profile of v0, /device:TPU:0, one launch (start us, length us, event | category | flops | bytes accessed | tf_op | source)
XLA Modules:
  0.0 323.4 jit_solution(6530451499667047419)
XLA Ops:
  7.2 0.0 copy-start
  7.2 0.0 reduce-scatter.2.cloned.1.call-start
  7.2 1.0 copy-done
  8.2 16.6 %convolution_convert_fusion = bf16[8192,128]{1,0:T(8,128)(2,1)} fusion(bf16[8192,2048]{1,0:T(8,128)(2,1)} %param.10, bf16[128,2048]{1,0:T(8,128)(2,1)S(1)} %copy-done), kind=kOutput, calls=%fused_computation.1 | convolution fusion | flops 4296015872 | bytes 36175872 | tf_op jit(solution)/shard_map/dot_general | solution.py:51
  24.8 0.0 reduce-scatter.2.cloned.1.call-update
  24.9 0.0 all-reduce.3.cloned.1.call-start
  24.9 0.1 pad.7.clone
  25.0 0.1 rev.6
  25.1 0.1 maximum_maximum_fusion
  25.2 0.1 copy.29
  25.3 0.3 copy.26
  25.6 7.1 %tile.4 = f32[128,128,257]{0,2,1:T(8,128)} broadcast(f32[128,257]{0,1:T(8,128)S(1)} %copy.29), dimensions={0,2} | broadcast | bytes 16974336 | tf_op jit(solution)/shard_map/tile | solution.py:27
  32.7 17.8 %tile.10 = f32[128,32896]{0,1:T(8,128)} reshape(f32[128,128,257]{0,2,1:T(8,128)} %tile.4) | data formatting | bytes 33685504 | tf_op jit(solution)/shard_map/tile | solution.py:27
  50.5 11.4 %slice.27 = f32[128,32768]{0,1:T(8,128)} slice(f32[128,32896]{0,1:T(8,128)} %tile.10), slice={[0:128], [0:32768]} | slice | bytes 33554432 | tf_op jit(solution)/shard_map/slice | solution.py:27
  61.9 17.7 %copy.36 = f32[128,128,256]{2,1,0:T(8,128)} copy(f32[128,128,256]{0,2,1:T(8,128)} %bitcast.44) | data formatting | bytes 33554432 | tf_op jit(solution)/shard_map/reshape | solution.py:28
  79.6 1.2 fusion.1
  80.7 0.0 copy-start.3
  80.8 7.2 %fusion.11 = f32[128,16,256]{2,1,0:T(8,128)S(1)} fusion(bf16[128,128,16]{0,2,1:T(8,128)(2,1)S(1)} %bitcast.52, f32[128,128,256]{2,1,0:T(8,128)} %copy.36), kind=kOutput, calls=%fused_computation.27 | convolution fusion | flops 138412032 | bytes 19398656 | tf_op jit(solution)/shard_map/gts,btgc->bsgc/dot_general | solution.py:38
  88.0 3.5 %copy-done.2 = f32[128,128,256]{2,1,0:T(8,128)S(1)} copy-done((f32[128,128,256]{2,1,0:T(8,128)S(1)}, f32[128,128,256]{2,1,0:T(8,128)}, u32[]{:S(2)}) %copy-start.2) | copy-done | bytes 16777240
  91.5 1.2 add_bitcast_fusion
  92.7 0.1 slice.33
  92.8 1.3 collective-permute-start.1
  94.1 15.5 %collective-permute-done.1 = bf16[128,2048]{0,1:T(8,128)(2,1)S(1)} collective-permute-done((bf16[128,2048]{0,1:T(8,128)(2,1)S(1)}, bf16[128,2048]{0,1:T(8,128)(2,1)S(1)}, u32[]{:S(2)}, u32[]{:S(2)}) %collective-permute-start.1) | collective-permute-done | bytes 524320 | tf_op jit(solution)/shard_map/ppermute | solution.py:12
  109.6 0.2 slice_add_fusion
  109.8 0.3 copy.31
  110.1 2.4 fusion.2
  112.5 4.7 %collective-permute-start = (bf16[128,2048]{1,0:T(8,128)(2,1)S(1)}, bf16[128,2048]{1,0:T(8,128)(2,1)S(1)}, u32[]{:S(2)}, u32[]{:S(2)}) collective-permute-start(bf16[128,2048]{1,0:T(8,128)(2,1)S(1)} %get-tuple-element.22), channel_id=1, source_target_pairs={{0,4},{4,8},{8,12},{12,16},{16,20},{20,24},{24,28},{1,5},{5,9},{9,... | collective-permute-start | bytes 1572872 | tf_op jit(solution)/shard_map/ppermute | solution.py:12
  117.2 0.3 copy.28
  117.5 9.7 %collective-permute-done = bf16[128,2048]{1,0:T(8,128)(2,1)S(1)} collective-permute-done((bf16[128,2048]{1,0:T(8,128)(2,1)S(1)}, bf16[128,2048]{1,0:T(8,128)(2,1)S(1)}, u32[]{:S(2)}, u32[]{:S(2)}) %collective-permute-start) | collective-permute-done | bytes 524320 | tf_op jit(solution)/shard_map/ppermute | solution.py:12
  127.2 0.3 copy.27
  127.5 9.2 %fusion.7 = f32[128,16,128]{2,1,0:T(8,128)} fusion(bf16[1,128,128,16]{1,3,2,0:T(8,128)(2,1)S(1)} %bitcast.46, bf16[1,128,128,16]{1,3,2,0:T(8,128)(2,1)S(1)} %bitcast.49, f32[128,128,256]{2,1,0:T(8,128)} %copy.36), kind=kOutput, calls=%fused_computation.21 | convolution fusion | flops 140509184 | bytes 18874368 | tf_op jit(solution)/shard_map/gts,bsgc->btgc/dot_general | solution.py:38
  136.8 8.2 %fusion.6 = f32[128,128,256]{2,1,0:T(8,128)} fusion(bf16[128,128,16]{0,2,1:T(8,128)(2,1)S(1)} %bitcast.54, bf16[1,128,128,16]{1,3,2,0:T(8,128)(2,1)S(1)} %bitcast.47, bf16[1,128,128,16]{1,3,2,0:T(8,128)(2,1)S(1)} %bitcast.50), kind=kOutput, calls=%fused_computation.20 | convolution fusion | flops 136314880 | bytes 18350080 | tf_op jit(solution)/shard_map/btgc,bsgc->gts/dot_general | solution.py:96
  145.0 4.5 %convolution_add_fusion = f32[128,16,128]{2,1,0:T(8,128)} fusion(f32[128,16,128]{2,1,0:T(8,128)} %fusion.7, bf16[1,128,128,16]{1,3,2,0:T(8,128)(2,1)S(1)} %bitcast.48, bf16[1,128,128,16]{1,3,2,0:T(8,128)(2,1)S(1)} %bitcast.51, f32[128,128,256]{2,1,0:T(8,128)S(1)} %bitcast.43), kind=kOutput, calls=%fused_computation.4 | convolution fusion | flops 153354240 | bytes 19922944 | tf_op jit(solution)/shard_map/gts,bsgc->btgc/dot_general | solution.py:39
  149.5 17.9 %copy.37 = f32[128,128,256]{0,2,1:T(8,128)} copy(f32[128,128,256]{2,1,0:T(8,128)} %fusion.6) | data formatting | bytes 33554432 | tf_op jit(solution)/shard_map/reshape | solution.py:99
  167.4 13.3 %pad.4 = f32[128,32896]{0,1:T(8,128)} pad(f32[128,32768]{0,1:T(8,128)} %bitcast.45, f32[]{:T(128)} %constant.2.clone.1), padding=0_0x0_128 | pad | bytes 33619972 | tf_op jit(solution)/shard_map/jit(_pad)/pad | solution.py:99
  180.7 17.5 %reshape.67 = f32[128,128,257]{0,2,1:T(8,128)} reshape(f32[128,32896]{0,1:T(8,128)} %pad.4) | data formatting | bytes 33685504 | tf_op jit(solution)/shard_map/reshape | solution.py:100
  198.2 6.9 %reduce_sum.9 = f32[128,257]{0,1:T(8,128)S(1)} reduce(f32[128,128,257]{0,2,1:T(8,128)} %reshape.67, f32[]{:T(128)} %constant.2.clone.1), dimensions={1}, to_apply=%region_1.2 | reduce | flops 4177792 | bytes 16974340 | tf_op jit(solution)/shard_map/reduce_sum | solution.py:100
  205.0 0.6 rev.7
  205.7 0.0 all-reduce.3.cloned.1.call-update
  205.7 0.3 all-gather.2.cloned.1.call-start
  206.0 1.0 fusion.5
  207.0 0.0 all-gather.2.cloned.1.call-update
  207.0 1.0 copy.34
  208.0 67.5 %all-reduce.3.cloned.1.call-done = f32[128,128]{0,1:T(8,128)} async-done(((f32[128,128]{0,1:T(8,128)}), f32[128,128]{0,1:T(8,128)}) %all-reduce.3.cloned.1.call-update) | async-done | bytes 65552 | tf_op jit(solution)/shard_map/psum | solution.py:102
  275.6 0.8 broadcast_multiply_fusion
  276.4 0.7 copy.35
  277.1 23.2 %all-gather.2.cloned.1.call-done = bf16[128,8192]{0,1:T(8,128)(2,1)} async-done(((bf16[128,2048]{0,1:T(8,128)(2,1)}), bf16[128,8192]{0,1:T(8,128)(2,1)}) %all-gather.2.cloned.1.call-update) | async-done | bytes 2097168 | tf_op jit(solution)/shard_map/all_gather | solution.py:76
  300.4 16.5 %convolution_convert_fusion.1 = bf16[128,2048]{1,0:T(8,128)(2,1)} fusion(bf16[128,8192]{0,1:T(8,128)(2,1)} %all-gather.2.cloned.1.call-done, bf16[8192,2048]{1,0:T(8,128)(2,1)} %param.10), kind=kOutput, calls=%fused_computation.2 | convolution fusion | flops 4295229440 | bytes 36175872 | tf_op jit(solution)/shard_map/dot_general | solution.py:75
  (33 shorter events, 0.1 us)
Async XLA Ops:
  7.2 1.1 copy-start
  7.2 17.8 %copy-start.11 = (f32[128,128]{1,0:T(8,128)S(1)}, f32[128,128]{1,0:T(8,128)}, u32[]{:S(2)}) copy-start(f32[128,128]{1,0:T(8,128)} %param.9) | copy-start | bytes 196612
  7.2 18.1 %copy-start.10 = (bf16[128,2048]{1,0:T(8,128)(2,1)S(1)}, bf16[128,2048]{1,0:T(8,128)(2,1)}, u32[]{:S(2)}) copy-start(bf16[128,2048]{1,0:T(8,128)(2,1)} %param.6) | copy-start | bytes 1572868
  7.2 72.4 %reduce-scatter.2.cloned.1.call-start = ((), (), s32[]{:S(2)}) async-start(), calls=%async_computation.2 | async-start | bytes 2621440 | tf_op jit(solution)/shard_map/reduce_scatter | solution.py:50
  24.9 250.7 %all-reduce.3.cloned.1.call-start = ((), (), s32[]{:S(2)}) async-start(), calls=%async_computation.3 | async-start | bytes 131072 | tf_op jit(solution)/shard_map/psum | solution.py:102
  25.6 54.0 %copy-start.5 = (bf16[128,2048]{0,1:T(8,128)(2,1)}, bf16[128,2048]{0,1:T(8,128)(2,1)S(1)}, u32[]{:S(2)}) copy-start(bf16[128,2048]{0,1:T(8,128)(2,1)S(1)} %copy.26) | copy-start | bytes 1572868
  80.7 7.2 %copy-start.3 = (bf16[128,2048]{0,1:T(8,128)(2,1)}, bf16[128,2048]{0,1:T(8,128)(2,1)S(1)}, u32[]{:S(2)}) copy-start(bf16[128,2048]{0,1:T(8,128)(2,1)S(1)} %fusion.1) | copy-start | bytes 1572868
  80.8 10.7 %copy-start.2 = (f32[128,128,256]{2,1,0:T(8,128)S(1)}, f32[128,128,256]{2,1,0:T(8,128)}, u32[]{:S(2)}) copy-start(f32[128,128,256]{2,1,0:T(8,128)} %copy.36) | copy-start | bytes 50331652
  91.5 18.6 %copy-start.9 = (bf16[128,2048]{1,0:T(8,128)(2,1)S(1)}, bf16[128,2048]{1,0:T(8,128)(2,1)}, u32[]{:S(2)}) copy-start(bf16[128,2048]{1,0:T(8,128)(2,1)} %param.7) | copy-start | bytes 1572868
  92.8 16.8 %collective-permute-start.1 = (bf16[128,2048]{0,1:T(8,128)(2,1)S(1)}, bf16[128,2048]{0,1:T(8,128)(2,1)S(1)}, u32[]{:S(2)}, u32[]{:S(2)}) collective-permute-start(bf16[128,2048]{0,1:T(8,128)(2,1)S(1)} %bitcast.57), channel_id=1, source_target_pairs={{4,0},{8,4},{12,8},{16,12},{20,16},{24,20},{28,24},{5,1},{9,5},{13... | collective-permute-start | bytes 1572872 | tf_op jit(solution)/shard_map/ppermute | solution.py:12
  112.5 14.7 %collective-permute-start = (bf16[128,2048]{1,0:T(8,128)(2,1)S(1)}, bf16[128,2048]{1,0:T(8,128)(2,1)S(1)}, u32[]{:S(2)}, u32[]{:S(2)}) collective-permute-start(bf16[128,2048]{1,0:T(8,128)(2,1)S(1)} %get-tuple-element.22), channel_id=1, source_target_pairs={{0,4},{4,8},{8,12},{12,16},{16,20},{20,24},{24,28},{1,5},{5,9},{9,... | collective-permute-start | bytes 1572872 | tf_op jit(solution)/shard_map/ppermute | solution.py:12
  127.5 9.3 %copy-start.4 = (bf16[128,2048]{0,1:T(8,128)(2,1)S(1)}, bf16[128,2048]{0,1:T(8,128)(2,1)}, u32[]{:S(2)}) copy-start(bf16[128,2048]{0,1:T(8,128)(2,1)} %copy-done.3) | copy-start | bytes 1572868
  127.5 17.4 %slice-start = ((s8[16777216]{0:T(1024)(128)(4,1)}), s8[4194304]{0:T(1024)(128)(4,1)S(1)}, s32[]{:S(2)}) async-start(s8[16777216]{0:T(1024)(128)(4,1)} %bitcast.42), calls=%async_computation.4 | async-start | bytes 8388608
  127.5 17.4 %slice-start.1 = ((s8[16777216]{0:T(1024)(128)(4,1)}), s8[4194304]{0:T(1024)(128)(4,1)S(1)}, s32[]{:S(2)}) async-start(s8[16777216]{0:T(1024)(128)(4,1)} %bitcast.42), calls=%async_computation.5 | async-start | bytes 8388608
  127.5 17.4 %slice-start.2 = ((s8[16777216]{0:T(1024)(128)(4,1)}), s8[4194304]{0:T(1024)(128)(4,1)S(1)}, s32[]{:S(2)}) async-start(s8[16777216]{0:T(1024)(128)(4,1)} %bitcast.42), calls=%async_computation.6 | async-start | bytes 8388608
  136.8 8.2 %slice-start.3 = ((s8[16777216]{0:T(1024)(128)(4,1)}), s8[4194304]{0:T(1024)(128)(4,1)S(1)}, s32[]{:S(2)}) async-start(s8[16777216]{0:T(1024)(128)(4,1)} %bitcast.42), calls=%async_computation.7 | async-start | bytes 8388608
  198.1 7.8 %copy-start.6 = (bf16[128,2048]{0,1:T(8,128)(2,1)S(1)}, bf16[128,2048]{0,1:T(8,128)(2,1)}, u32[]{:S(2)}) copy-start(bf16[128,2048]{0,1:T(8,128)(2,1)} %copy-done.5) | copy-start | bytes 1572868
  198.1 7.8 %copy-start.7 = (f32[128,16,128]{2,1,0:T(8,128)S(1)}, f32[128,16,128]{2,1,0:T(8,128)}, u32[]{:S(2)}) copy-start(f32[128,16,128]{2,1,0:T(8,128)} %convolution_add_fusion) | copy-start | bytes 3145732
  198.2 7.8 %copy-start.8 = (bf16[2048,128]{1,0:T(8,128)(2,1)S(1)}, bf16[2048,128]{1,0:T(8,128)(2,1)}, u32[]{:S(2)}) copy-start(bf16[2048,128]{1,0:T(8,128)(2,1)} %reduce-scatter.2.cloned.1.call-done) | copy-start | bytes 1572868
  205.7 94.6 %all-gather.2.cloned.1.call-start = ((), (), s32[]{:S(2)}) async-start(), calls=%async_computation.1 | async-start | bytes 2621440 | tf_op jit(solution)/shard_map/all_gather | solution.py:76
  300.3 16.5 %copy-start.1 = (bf16[128,2048]{1,0:T(8,128)(2,1)S(1)}, bf16[128,2048]{1,0:T(8,128)(2,1)}, u32[]{:S(2)}) copy-start(bf16[128,2048]{1,0:T(8,128)(2,1)} %param.11) | copy-start | bytes 1572868
Sparse Core Ops, SparseCore 0:
  25.0 34.1 reduce-scatter.1
  205.8 69.7 all-reduce.2
  277.8 22.5 all-gather.1
where the time goes:
time: 325 us; the launch traced here: 323 us
  waiting for transfers between devices  116 us (36%)
  local copies, waits for them, and re-layouts  111 us (34%)
  matrix products  63.5 us (20%)
  between operations  14 us (4%)
  other arithmetic  12.5 us (4%)
  starting transfers between devices  6.37 us (2%)
    psum x1, waiting for transfers between devices, local(): summed = lax.psum(local_terms, 'tok')  67.5 us
    ppermute x2, waiting for transfers between devices, shifted(): return lax.ppermute(block, axis, route)  25.2 us
    another operation x2, local copies, waits for them, and re-layouts, causal_matrix(): tiled = jnp.tile(padded, (1, kernel))[:, :kernel * span]  24.9 us
    all_gather x1, waiting for transfers between devices, local(): lax.all_gather(gated, 'wid', axis=1, tiled=True)  23.2 us
    reshape x1, local copies, waits for them, and re-layouts, local(): products.reshape(groups, kernel * 2 * kernel)  17.9 us
    reshape x1, local copies, waits for them, and re-layouts, causal_matrix(): return tiled.reshape(groups, kernel, span)  17.7 us
    reshape x1, local copies, waits for them, and re-layouts, local(): skewed = flat.reshape(groups, kernel, 2 * kernel + 1).sum(axis=1)  17.5 us
    dot_general x1, matrix products, gated_gradient(): lax.dot_general(out_weight, cotangent, (((1,), (1,)), ((), ())), preferre...  16.6 us
  transfers between devices with their start and end apart: 5, of which 4 were waited for; matrix products, arithmetic and copies ran while one was open for 18% of the time, Pallas kernels for 0%

commit v1 on v0

v1 whole, which is shorter than its diff:
```python
import functools
import math

import jax
import jax.numpy as jnp
from jax import lax
from jax.experimental import pallas as pl
from jax.experimental.pallas import tpu as pltpu
from jax.sharding import PartitionSpec as P


def shifted(block, axis, distance):
    devices = range(lax.axis_size(axis))
    route = [(i - distance, i) for i in devices if i - distance in devices]
    return lax.ppermute(block, axis, route)


def iota(shape, dim):
    return lax.broadcasted_iota(jnp.int32, shape, dim)


def circulant(row, kernel):
    return pltpu.roll(jnp.broadcast_to(row, (kernel, kernel)), 0, 1, stride=1, stride_axis=0)


def forward_tile(filters_rev, extended, group_size):
    groups, kernel = filters_rev.shape
    tile = extended.shape[1]
    row, lane = iota((kernel, kernel), 0), iota((kernel, kernel), 1)
    now = lane <= row
    owner = iota((kernel, tile), 1) // group_size
    result = jnp.zeros((kernel, tile), jnp.float32)
    for g in range(groups):
        ring = circulant(filters_rev[g : g + 1], kernel)
        both = jnp.concatenate(
            [jnp.where(now, 0.0, ring).astype(jnp.bfloat16), jnp.where(now, ring, 0.0).astype(jnp.bfloat16)],
            axis=1,
        )
        part = jnp.dot(both, extended, preferred_element_type=jnp.float32)
        result = jnp.where(owner == g, part, result)
    return result


def backward_tile(filters, grads, group_size):
    groups, kernel = filters.shape
    tile = grads.shape[1]
    row, lane = iota((kernel, kernel), 0), iota((kernel, kernel), 1)
    now = row <= lane
    owner = iota((kernel, tile), 1) // group_size
    result = jnp.zeros((kernel, tile), jnp.float32)
    for g in range(groups):
        ring = circulant(filters[g : g + 1], kernel)
        both = jnp.concatenate(
            [jnp.where(now, ring, 0.0).astype(jnp.bfloat16), jnp.where(now, 0.0, ring).astype(jnp.bfloat16)],
            axis=1,
        )
        part = jnp.dot(both, grads, preferred_element_type=jnp.float32)
        result = jnp.where(owner == g, part, result)
    return result


def filter_tile(extended, own_grads, groups, group_size):
    kernel, tile = own_grads.shape
    row, lane = iota((kernel, kernel), 0), iota((kernel, kernel), 1)
    now = row + lane >= kernel - 1
    owner = iota((2 * kernel, tile), 1) // group_size
    mirror = jnp.where(row + lane == kernel - 1, 1.0, 0.0).astype(jnp.bfloat16)
    extended = jnp.concatenate(
        [
            jnp.dot(mirror, half, preferred_element_type=jnp.float32).astype(jnp.bfloat16)
            for half in (extended[:kernel], extended[kernel:])
        ],
        axis=0,
    )
    rows = []
    for g in range(groups):
        part = lax.dot_general(
            jnp.where(owner == g, extended, jnp.zeros_like(extended)),
            own_grads,
            (((1,), (1,)), ((), ())),
            preferred_element_type=jnp.float32,
        )
        square = jnp.where(now, part[kernel:], part[:kernel])
        aligned = pltpu.roll(square, 1, 1, stride=1, stride_axis=0)
        rows.append(jnp.sum(aligned, axis=0, keepdims=True))
    return jnp.concatenate(rows, axis=0)


def forward_kernel(group_size, q_ref, kv_ref, rim_ref, filters_rev_ref, conv_ref, gated_ref):
    extended = jnp.concatenate([rim_ref[...], kv_ref[...]], axis=0)
    conv = forward_tile(filters_rev_ref[...], extended, group_size)
    conv_ref[...] = conv
    gated_ref[...] = (q_ref[...].astype(jnp.float32) * conv).astype(jnp.bfloat16)


def backward_kernel(
    group_size, k_ref, v_ref, rim_ref, gc_ref, gc_next_ref, filters_ref, gk_ref, gv_ref, gf_ref
):
    key, value = k_ref[...].astype(jnp.float32), v_ref[...].astype(jnp.float32)
    kv = (key * value).astype(jnp.bfloat16)
    extended = jnp.concatenate([rim_ref[...], kv], axis=0)
    own = gc_ref[...]
    filters = filters_ref[...]
    grad_kv = backward_tile(filters, jnp.concatenate([own, gc_next_ref[...]], axis=0), group_size)
    gk_ref[...] = (grad_kv * value).astype(jnp.bfloat16)
    gv_ref[...] = (grad_kv * key).astype(jnp.bfloat16)
    gf_ref[...] = filter_tile(extended, own, filters.shape[0], group_size)


def local(queries, key_branch, value_branch, filters, out_weight, cotangent):
    length, width = queries.shape
    groups, kernel = filters.shape
    group_size = width // groups
    tile = min(256, width)
    tile_groups = tile // group_size
    channels = pl.BlockSpec((length, tile), lambda i: (0, i))
    by_group = pl.BlockSpec((tile_groups, kernel), lambda i: (i, 0))
    wide = jax.ShapeDtypeStruct((length, width), jnp.bfloat16)
    flops = 2 * width * tile_groups * kernel * 2 * kernel

    kv = (key_branch.astype(jnp.float32) * value_branch.astype(jnp.float32)).astype(jnp.bfloat16)
    rim = shifted(kv, "tok", 1)
    partial = lax.dot_general(
        out_weight, cotangent, (((1,), (1,)), ((), ())), preferred_element_type=jnp.float32
    ).astype(jnp.bfloat16)
    filters_rev = jnp.roll(filters[:, ::-1], 1, axis=1)
    conv, gated = pl.pallas_call(
        functools.partial(forward_kernel, group_size),
        grid=(width // tile,),
        in_specs=[channels, channels, channels, by_group],
        out_specs=[channels, channels],
        out_shape=[jax.ShapeDtypeStruct((length, width), jnp.float32), wide],
        cost_estimate=pl.CostEstimate(flops=flops, bytes_accessed=10 * length * width, transcendentals=0),
    )(queries, kv, rim, filters_rev)
    grad_gated = (
        lax.psum_scatter(partial, "wid", scatter_dimension=0, tiled=True).astype(jnp.float32).T
    )
    layer_out = jnp.dot(
        lax.all_gather(gated, "wid", axis=1, tiled=True),
        out_weight,
        preferred_element_type=jnp.float32,
    ).astype(jnp.bfloat16)
    grad_conv = (grad_gated * queries.astype(jnp.float32)).astype(jnp.bfloat16)
    grad_queries = (grad_gated * conv).astype(jnp.bfloat16)
    grad_next = shifted(grad_conv, "tok", -1)
    grad_keys, grad_values, local_terms = pl.pallas_call(
        functools.partial(backward_kernel, group_size),
        grid=(width // tile,),
        in_specs=[channels] * 5 + [by_group],
        out_specs=[channels, channels, by_group],
        out_shape=[wide, wide, jax.ShapeDtypeStruct((groups, kernel), jnp.float32)],
        cost_estimate=pl.CostEstimate(flops=2 * flops, bytes_accessed=14 * length * width, transcendentals=0),
    )(key_branch, value_branch, rim, grad_conv, grad_next, filters)
    scale_factor = 1.0 / math.sqrt(length * lax.axis_size("tok") * group_size)
    grad_filters = lax.psum(local_terms, "tok") * scale_factor
    return (layer_out, grad_queries, grad_keys, grad_values, grad_filters)


def solution(mesh):
    return jax.shard_map(
        local,
        mesh=mesh,
        in_specs=(
            P("tok", "wid"),
            P("tok", "wid"),
            P("tok", "wid"),
            P("wid", None),
            P(None, "wid"),
            P("tok", "wid"),
        ),
        out_specs=(
            P("tok", "wid"),
            P("tok", "wid"),
            P("tok", "wid"),
            P("tok", "wid"),
            P("wid", None),
        ),
        check_vma=False,
    )
```

time: 325 us -> 174 us (0.54)
  local copies, waits for them, and re-layouts: 111 us -> 2.73 us
  waiting for transfers between devices: 116 us -> 86.3 us
  matrix products: 63.5 us -> 39.5 us
  Pallas kernels: 0 us -> 19.2 us
  other arithmetic: 12.5 us -> 4.78 us
    reshape x4 -> x0, local copies, waits for them, and re-layouts: 53.3 us -> none  [the longest x1 17.9 us: local(): products.reshape(groups, kernel * 2 * kernel)]
    another operation x2 -> x0, local copies, waits for them, and re-layouts: 24.9 us -> none  [causal_matrix(): tiled = jnp.tile(padded, (1, kernel))[:, :kernel * span]]
    dot_general x6 -> x1, matrix products: 47 us -> 23 us  [local(): lax.dot_general(out_weight, cotangent, (((1,), (1,)), ((), ())), preferre...]
    all_gather x1, waiting for transfers between devices: 23.2 us -> 0.02 us  [local(): lax.all_gather(gated, 'wid', axis=1, tiled=True)]
    pallas_call x0 -> x2, Pallas kernels: none -> 19.2 us  [the longest x1 11.9 us: local(): pl.pallas_call(functools.partial(backward_kernel, group_size), grid=(widt...]
    psum x1, waiting for transfers between devices: 67.5 us -> 52.1 us  [local(): grad_filters = lax.psum(local_terms, 'tok') * scale_factor]
    pad x1 -> x0, local copies, waits for them, and re-layouts: 13.3 us -> none  [local(): jnp.pad(products.reshape(groups, kernel * 2 * kernel), ((0, 0), (0, kerne...]
    slice x3 -> x2, local copies, waits for them, and re-layouts: 11.5 us -> 0.16 us  [local(): filters_rev = jnp.roll(filters[:, ::-1], 1, axis=1)]
  transfers between devices with their start and end apart: 5 -> 5, of which waited for: 4 -> 4; matrix products, arithmetic and copies ran while one was open for 18% -> 12% of each run, Pallas kernels for 0% -> 11%
where the time goes in v1:
time: 174 us; the launch traced here: 173 us
  waiting for transfers between devices  86.3 us (50%)
  matrix products  39.5 us (23%)
  Pallas kernels  19.2 us (11%)
  between operations  13.9 us (8%)
  starting transfers between devices  6.48 us (4%)
  other arithmetic  4.78 us (3%)
  local copies, waits for them, and re-layouts  2.73 us (2%)
    psum x1, waiting for transfers between devices, local(): grad_filters = lax.psum(local_terms, 'tok') * scale_factor  52.1 us
    ppermute x2, waiting for transfers between devices, shifted(): return lax.ppermute(block, axis, route)  24.3 us
    dot_general x1, matrix products, local(): lax.dot_general(out_weight, cotangent, (((1,), (1,)), ((), ())), preferre...  23 us
    dot_general x1, matrix products, local(): jnp.dot(lax.all_gather(gated, 'wid', axis=1, tiled=True), out_weight, pre...  16.5 us
    pallas_call x1, Pallas kernels, local(): pl.pallas_call(functools.partial(backward_kernel, group_size), grid=(widt...  11.9 us
    reduce_scatter x1, waiting for transfers between devices, local(): lax.psum_scatter(partial, 'wid', scatter_dimension=0, tiled=True)  9.85 us
    pallas_call x1, Pallas kernels, local(): pl.pallas_call(functools.partial(forward_kernel, group_size), grid=(width...  7.31 us
    ppermute x2, starting transfers between devices, shifted(): return lax.ppermute(block, axis, route)  6.36 us
  transfers between devices with their start and end apart: 5, of which 4 were waited for; matrix products, arithmetic and copies ran while one was open for 12% of the time, Pallas kernels for 11%

profile of v1, /device:TPU:0, one launch (start us, length us, event | category | flops | bytes accessed | tf_op | source)
XLA Modules:
  0.0 172.8 jit_solution(10701889733907727710)
XLA Ops:
  7.2 0.0 copy-start
  7.2 0.0 copy-start.1
  7.2 0.0 copy-start.2
  7.2 0.0 copy-start.6
  7.2 0.0 copy-start.4
  7.2 0.0 reduce-scatter.2.cloned.1.call-start
  7.3 0.9 copy-done
  8.2 23.0 %convolution_convert_fusion = bf16[8192,128]{0,1:T(8,128)(2,1)} fusion(bf16[8192,2048]{1,0:T(8,128)(2,1)} %param.10, bf16[128,2048]{1,0:T(8,128)(2,1)S(1)} %copy-done), kind=kOutput, calls=%fused_computation | convolution fusion | flops 4296015872 | bytes 36175872 | tf_op jit(solution)/shard_map/dot_general | solution.py:123
  31.2 0.0 reduce-scatter.2.cloned.1.call-update
  31.2 0.0 all-gather.2.cloned.1.call-start
  31.3 0.0 copy-done.1
  31.3 0.0 copy-done.2
  31.3 0.1 multiply_convert_fusion.kv_ref
  31.4 0.0 copy-start.3
  31.4 4.9 %collective-permute-start = (bf16[128,2048]{1,0:T(8,128)(2,1)S(1)}, bf16[128,2048]{1,0:T(8,128)(2,1)S(1)}, u32[]{:S(2)}, u32[]{:S(2)}) collective-permute-start(bf16[128,2048]{1,0:T(8,128)(2,1)S(1)} %multiply_convert_fusion.kv_ref), channel_id=1, source_target_pairs={{0,4},{4,8},{8,12},{12,16},{16,20},{20,24},{24,28},{1,5},{5,9},{9,... | collective-permute-start | bytes 1572872 | tf_op jit(solution)/shard_map/ppermute | solution.py:15
  36.4 0.0 copy-done.6
  36.4 0.1 slice.13
  36.4 0.1 slice.14
  36.5 0.7 pad_maximum_fusion.filters_rev_ref
  37.3 10.2 %collective-permute-done.rim_ref = bf16[128,2048]{1,0:T(8,128)(2,1)S(1)} collective-permute-done((bf16[128,2048]{1,0:T(8,128)(2,1)S(1)}, bf16[128,2048]{1,0:T(8,128)(2,1)S(1)}, u32[]{:S(2)}, u32[]{:S(2)}) %collective-permute-start) | collective-permute-done | bytes 524320 | tf_op jit(solution)/shard_map/ppermute | solution.py:15
  47.5 0.0 copy-done.3
  47.5 0.0 copy-start.7
  47.5 0.8 copy-done.7
  48.3 7.3 %shard_map.101 = (f32[128,2048]{1,0:T(8,128)}, bf16[128,2048]{1,0:T(8,128)(2,1)}) custom-call(bf16[128,2048]{1,0:T(8,128)(2,1)} %q_ref.1, bf16[128,2048]{1,0:T(8,128)(2,1)} %copy-done.3, bf16[128,2048]{1,0:T(8,128)(2,1)} %copy-done.7, f32[128,128]{1,0:T(8,128)} %pad_maximum_fusion.filters_rev_ref), custom_call_target="tpu_custom_call" | custom-call | flops 2147483648 | bytes 2621440 | tf_op jit(solution)/shard_map/pallas_call | solution.py:127
  55.6 0.0 all-gather.2.cloned.1.call-update
  55.6 0.0 all-reduce.2.cloned.1.call-start
  55.7 9.9 %reduce-scatter.2.cloned.1.call-done = bf16[2048,128]{0,1:T(8,128)(2,1)} async-done(((bf16[8192,128]{0,1:T(8,128)(2,1)}), bf16[2048,128]{0,1:T(8,128)(2,1)}) %reduce-scatter.2.cloned.1.call-update) | async-done | bytes 524304 | tf_op jit(solution)/shard_map/reduce_scatter | solution.py:136
  65.5 0.0 copy-done.4
  65.5 2.4 %fusion.1 = (bf16[128,2048]{1,0:T(8,128)(2,1)S(1)}, bf16[128,2048]{1,0:T(8,128)(2,1)}) fusion(bf16[2048,128]{0,1:T(8,128)(2,1)} %reduce-scatter.2.cloned.1.call-done, bf16[128,2048]{1,0:T(8,128)(2,1)S(1)} %copy-done.4, f32[128,2048]{1,0:T(8,128)} %get-tuple-element.11), kind=kLoop, calls=%fused_computation.5 | loop fusion | flops 1572864 | bytes 3145728 | tf_op jit(solution)/shard_map/convert_element_type | solution.py:143
  68.0 0.0 copy-start.5
  68.0 1.5 collective-permute-start.1
  69.4 14.1 %collective-permute-done.1.gc_next_ref = bf16[128,2048]{1,0:T(8,128)(2,1)S(1)} collective-permute-done((bf16[128,2048]{1,0:T(8,128)(2,1)S(1)}, bf16[128,2048]{1,0:T(8,128)(2,1)S(1)}, u32[]{:S(2)}, u32[]{:S(2)}) %collective-permute-start.1) | collective-permute-done | bytes 524320 | tf_op jit(solution)/shard_map/ppermute | solution.py:15
  83.5 0.0 copy-done.5
  83.5 0.0 copy-start.8
  83.5 0.8 copy-done.8
  84.3 11.9 %shard_map.102 = (bf16[128,2048]{1,0:T(8,128)(2,1)}, bf16[128,2048]{1,0:T(8,128)(2,1)}, f32[128,128]{1,0:T(8,128)}) custom-call(bf16[128,2048]{1,0:T(8,128)(2,1)} %k_ref.1, bf16[128,2048]{1,0:T(8,128)(2,1)} %v_ref.1, bf16[128,2048]{1,0:T(8,128)(2,1)} %copy-done.7, bf16[128,2048]{1,0:T(8,128)(2,1)} %copy-done.5, bf16[128,2048]{1,0:T(8,128)(2,1)} %copy-done.8, ...), custom_call_target="tpu_custom_call" | custom-call | flops 4294967296 | bytes 3670016 | tf_op jit(solution)/shard_map/pallas_call | solution.py:146
  96.2 0.0 all-reduce.2.cloned.1.call-update
  96.2 0.0 all-gather.2.cloned.1.call-done
  96.2 16.5 %convolution_convert_fusion.1 = bf16[128,2048]{1,0:T(8,128)(2,1)} fusion(bf16[128,8192]{1,0:T(8,128)(2,1)} %all-gather.2.cloned.1.call-done, bf16[8192,2048]{1,0:T(8,128)(2,1)} %param.10), kind=kOutput, calls=%fused_computation.1 | convolution fusion | flops 4295229440 | bytes 36175872 | tf_op jit(solution)/shard_map/dot_general | solution.py:138
  112.8 52.1 %all-reduce.2.cloned.1.call-done = f32[128,128]{1,0:T(8,128)} async-done(((f32[128,128]{1,0:T(8,128)}), f32[128,128]{1,0:T(8,128)}) %all-reduce.2.cloned.1.call-update) | async-done | bytes 65552 | tf_op jit(solution)/shard_map/psum | solution.py:155
  164.8 1.5 broadcast_multiply_fusion
Async XLA Ops:
  7.2 1.0 copy-start
  7.2 24.1 %copy-start.1 = (bf16[128,2048]{1,0:T(8,128)(2,1)S(1)}, bf16[128,2048]{1,0:T(8,128)(2,1)}, u32[]{:S(2)}) copy-start(bf16[128,2048]{1,0:T(8,128)(2,1)} %v_ref.1) | copy-start | bytes 1572868
  7.2 24.1 %copy-start.2 = (bf16[128,2048]{1,0:T(8,128)(2,1)S(1)}, bf16[128,2048]{1,0:T(8,128)(2,1)}, u32[]{:S(2)}) copy-start(bf16[128,2048]{1,0:T(8,128)(2,1)} %k_ref.1) | copy-start | bytes 1572868
  7.2 29.2 %copy-start.6 = (f32[128,128]{1,0:T(8,128)S(1)}, f32[128,128]{1,0:T(8,128)}, u32[]{:S(2)}) copy-start(f32[128,128]{1,0:T(8,128)} %filters_ref.1) | copy-start | bytes 196612
  7.2 58.3 %copy-start.4 = (bf16[128,2048]{1,0:T(8,128)(2,1)S(1)}, bf16[128,2048]{1,0:T(8,128)(2,1)}, u32[]{:S(2)}) copy-start(bf16[128,2048]{1,0:T(8,128)(2,1)} %q_ref.1) | copy-start | bytes 1572868
  7.2 58.3 %reduce-scatter.2.cloned.1.call-start = ((), (), s32[]{:S(2)}) async-start(), calls=%async_computation.2 | async-start | bytes 2621440 | tf_op jit(solution)/shard_map/reduce_scatter | solution.py:136
  31.2 65.0 %all-gather.2.cloned.1.call-start = ((), (), s32[]{:S(2)}) async-start(), calls=%async_computation.1 | async-start | bytes 2621440 | tf_op jit(solution)/shard_map/all_gather | solution.py:139
  31.4 16.1 %copy-start.3 = (bf16[128,2048]{1,0:T(8,128)(2,1)}, bf16[128,2048]{1,0:T(8,128)(2,1)S(1)}, u32[]{:S(2)}) copy-start(bf16[128,2048]{1,0:T(8,128)(2,1)S(1)} %multiply_convert_fusion.kv_ref) | copy-start | bytes 1572868
  31.4 16.0 %collective-permute-start = (bf16[128,2048]{1,0:T(8,128)(2,1)S(1)}, bf16[128,2048]{1,0:T(8,128)(2,1)S(1)}, u32[]{:S(2)}, u32[]{:S(2)}) collective-permute-start(bf16[128,2048]{1,0:T(8,128)(2,1)S(1)} %multiply_convert_fusion.kv_ref), channel_id=1, source_target_pairs={{0,4},{4,8},{8,12},{12,16},{16,20},{20,24},{24,28},{1,5},{5,9},{9,... | collective-permute-start | bytes 1572872 | tf_op jit(solution)/shard_map/ppermute | solution.py:15
  47.5 0.8 copy-start.7
  55.6 109.2 %all-reduce.2.cloned.1.call-start = ((), (), s32[]{:S(2)}) async-start(), calls=%async_computation.3 | async-start | bytes 131072 | tf_op jit(solution)/shard_map/psum | solution.py:155
  68.0 15.6 %copy-start.5 = (bf16[128,2048]{1,0:T(8,128)(2,1)}, bf16[128,2048]{1,0:T(8,128)(2,1)S(1)}, u32[]{:S(2)}) copy-start(bf16[128,2048]{1,0:T(8,128)(2,1)S(1)} %get-tuple-element.15.gc_ref) | copy-start | bytes 1572868
  68.0 15.5 %collective-permute-start.1 = (bf16[128,2048]{1,0:T(8,128)(2,1)S(1)}, bf16[128,2048]{1,0:T(8,128)(2,1)S(1)}, u32[]{:S(2)}, u32[]{:S(2)}) collective-permute-start(bf16[128,2048]{1,0:T(8,128)(2,1)S(1)} %get-tuple-element.15.gc_ref), channel_id=1, source_target_pairs={{4,0},{8,4},{12,8},{16,12},{20,16},{24,20},{28,24},{5,1},{9,5},{13... | collective-permute-start | bytes 1572872 | tf_op jit(solution)/shard_map/ppermute | solution.py:15
  83.5 0.8 copy-start.8
Sparse Core Ops, SparseCore 0:
  31.4 34.1 reduce-scatter.1
  67.2 22.5 all-gather.1
  96.3 68.4 all-reduce.1

commit v2 on v1

v2 whole, which is shorter than its diff:
```python
import functools
import math

import jax
import jax.numpy as jnp
from jax import lax
from jax.experimental import pallas as pl
from jax.experimental.pallas import tpu as pltpu
from jax.sharding import PartitionSpec as P


def iota(shape, dim):
    return lax.broadcasted_iota(jnp.int32, shape, dim)


def circulant(row, kernel):
    return pltpu.roll(jnp.broadcast_to(row, (kernel, kernel)), 0, 1, stride=1, stride_axis=0)


def forward_tile(filters_rev, extended, group_size):
    groups, kernel = filters_rev.shape
    tile = extended.shape[1]
    row, lane = iota((kernel, kernel), 0), iota((kernel, kernel), 1)
    now = lane <= row
    owner = iota((kernel, tile), 1) // group_size
    result = jnp.zeros((kernel, tile), jnp.float32)
    for g in range(groups):
        ring = circulant(filters_rev[g : g + 1], kernel)
        both = jnp.concatenate(
            [jnp.where(now, 0.0, ring).astype(jnp.bfloat16), jnp.where(now, ring, 0.0).astype(jnp.bfloat16)],
            axis=1,
        )
        part = jnp.dot(both, extended, preferred_element_type=jnp.float32)
        result = jnp.where(owner == g, part, result)
    return result


def backward_tile(filters, grads, group_size):
    groups, kernel = filters.shape
    tile = grads.shape[1]
    row, lane = iota((kernel, kernel), 0), iota((kernel, kernel), 1)
    now = row <= lane
    owner = iota((kernel, tile), 1) // group_size
    result = jnp.zeros((kernel, tile), jnp.float32)
    for g in range(groups):
        ring = circulant(filters[g : g + 1], kernel)
        both = jnp.concatenate(
            [jnp.where(now, ring, 0.0).astype(jnp.bfloat16), jnp.where(now, 0.0, ring).astype(jnp.bfloat16)],
            axis=1,
        )
        part = jnp.dot(both, grads, preferred_element_type=jnp.float32)
        result = jnp.where(owner == g, part, result)
    return result


def filter_tile(extended, own_grads, groups, group_size):
    kernel, tile = own_grads.shape
    row, lane = iota((kernel, kernel), 0), iota((kernel, kernel), 1)
    now = row + lane >= kernel - 1
    owner = iota((2 * kernel, tile), 1) // group_size
    mirror = jnp.where(row + lane == kernel - 1, 1.0, 0.0).astype(jnp.bfloat16)
    extended = jnp.concatenate(
        [
            jnp.dot(mirror, half, preferred_element_type=jnp.float32).astype(jnp.bfloat16)
            for half in (extended[:kernel], extended[kernel:])
        ],
        axis=0,
    )
    rows = []
    for g in range(groups):
        part = lax.dot_general(
            jnp.where(owner == g, extended, jnp.zeros_like(extended)),
            own_grads,
            (((1,), (1,)), ((), ())),
            preferred_element_type=jnp.float32,
        )
        square = jnp.where(now, part[kernel:], part[:kernel])
        aligned = pltpu.roll(square, 1, 1, stride=1, stride_axis=0)
        rows.append(jnp.sum(aligned, axis=0, keepdims=True))
    return jnp.concatenate(rows, axis=0)


def kernel(
    sizes,
    q_ref, k_ref, v_ref, f_ref, w_ref, cot_ref,
    out_ref, gq_ref, gk_ref, gv_ref, gf_ref,
    w_buf, kv_buf, rim_buf, conv_buf, part_buf, sib_out, sib_in, pre_out, pre_in,
    gather, total, gc_buf, gcn_buf, frev_buf, local_buf, terms_buf, all_buf,
    w_sem, kv_send, kv_recv, sib_send, sib_recv, pre_send, pre_recv,
    own_send, own_recv, peer_send, peer_recv, fwd_send, fwd_recv, gc_send, gc_recv,
    term_send, term_recv, sum_send, sum_recv,
):
    n_tok, n_wid, tile, chunk, halves, owners = sizes
    length, width = q_ref.shape
    groups, kernel_size = f_ref.shape
    group_size = width // groups
    tile_groups = tile // group_size
    per_block = width // chunk
    chips = n_wid // 2
    rows = groups // owners
    half = width // halves
    tok, me = lax.axis_index("tok"), lax.axis_index("wid")
    chip, core = me // 2, lax.rem(me, 2)
    sibling = chip * 2 + 1 - core
    other_chips = [lax.rem(chip + off, chips) for off in range(1, chips)]
    other_toks = [lax.rem(tok + off, n_tok) for off in range(1, n_tok)]
    order = []
    for p in other_chips + [chip]:
        order += [p * 2 + 1 - core, p * 2 + core]

    def w_copy(position, j):
        at = pl.ds(pl.multiple_of(order[position] * width + j * chunk, chunk), chunk)
        return pltpu.make_async_copy(w_ref.at[at], w_buf.at[at], w_sem.at[position * per_block + j])

    for position in range(n_wid):
        for j in range(per_block):
            w_copy(position, j).start()

    def remote(src, dst, send, recv, **where):
        return pltpu.make_async_remote_copy(
            src_ref=src, dst_ref=dst, send_sem=send, recv_sem=recv,
            device_id=where, device_id_type=pl.DeviceIdType.MESH,
        )

    barrier = pltpu.get_barrier_semaphore()
    for where in (
        [{"wid": sibling}] + [{"wid": p * 2 + core} for p in other_chips] + [{"tok": t} for t in other_toks]
    ):
        pl.semaphore_signal(barrier, inc=1, device_id=where, device_id_type=pl.DeviceIdType.MESH)
    pl.semaphore_wait(barrier, 1 + len(other_chips) + len(other_toks))

    kv_buf[...] = (k_ref[...].astype(jnp.float32) * v_ref[...].astype(jnp.float32)).astype(jnp.bfloat16)
    kv_copy = remote(kv_buf, rim_buf, kv_send, kv_recv, tok=lax.rem(tok + 1, n_tok))
    has_next, has_previous = tok < n_tok - 1, tok > 0

    @pl.when(has_next)
    def _():
        kv_copy.start()

    cot = cot_ref[...]

    def sib_copy(p):
        return remote(sib_out.at[p], sib_in.at[p], sib_send.at[p], sib_recv.at[p], wid=sibling)

    def pre_copy(p, slot):
        return remote(pre_out.at[p], pre_in.at[slot], pre_send.at[p], pre_recv.at[slot], wid=p * 2 + core)

    for position in range(n_wid):
        block = order[position]

        @pl.loop(0, per_block)
        def _(j):
            w_copy(position, j).wait()
            at = pl.ds(pl.multiple_of(block * width + j * chunk, chunk), chunk)
            part_buf[:, pl.ds(pl.multiple_of(j * chunk, chunk), chunk)] = lax.dot_general(
                cot, w_buf[at, :], (((1,), (1,)), ((), ())), preferred_element_type=jnp.float32
            )

        p = (other_chips + [chip])[position // 2]
        if position % 2 == 0:
            sib_out[p] = part_buf[...].astype(jnp.bfloat16)
            sib_copy(p).start()
        elif position < n_wid - 1:
            sib_copy(p).wait_recv()
            pre_out[p] = (part_buf[...] + sib_in[p].astype(jnp.float32)).astype(jnp.bfloat16)
            pre_copy(p, chip).start()

    flip = jnp.where(
        lax.rem(iota((kernel_size, kernel_size), 0) + iota((kernel_size, kernel_size), 1), kernel_size) == 0, 1.0, 0.0
    ).astype(jnp.bfloat16)
    frev_buf[...] = jnp.dot(f_ref[...].astype(jnp.bfloat16), flip, preferred_element_type=jnp.float32)

    @pl.when(has_previous)
    def _():
        kv_copy.wait_recv()

    @pl.when(jnp.logical_not(has_previous))
    def _():
        rim_buf[...] = jnp.zeros_like(rim_buf)

    def own_copy(h, slot):
        at = pl.ds(h * half, half)
        return remote(gather.at[me, :, at], gather.at[slot, :, at], own_send.at[h], own_recv.at[h], wid=sibling)

    def peer_copy(p, h, slot, slot_chip):
        at = pl.ds(h * half, half)
        return remote(
            gather.at[me, :, at], gather.at[slot, :, at],
            peer_send.at[p * halves + h], peer_recv.at[slot_chip * halves + h], wid=p * 2 + core,
        )

    def fwd_copy(p, h, slot):
        at = pl.ds(h * half, half)
        return remote(
            gather.at[p * 2 + core, :, at], gather.at[slot, :, at],
            fwd_send.at[p * halves + h], fwd_recv.at[p * halves + h], wid=sibling,
        )

    for h in range(halves):

        @pl.loop(h * (half // tile), (h + 1) * (half // tile))
        def _(i):
            at = pl.ds(pl.multiple_of(i * tile, tile), tile)
            which = pl.ds(pl.multiple_of(i * tile_groups, tile_groups), tile_groups)
            extended = jnp.concatenate([rim_buf[:, at], kv_buf[:, at]], axis=0)
            conv = forward_tile(frev_buf[which, :], extended, group_size)
            conv_buf[:, at] = conv
            gather[me, :, at] = (q_ref[:, at].astype(jnp.float32) * conv).astype(jnp.bfloat16)

        for p in other_chips:
            peer_copy(p, h, me, chip).start()
        own_copy(h, me).start()

    sib_copy(chip).wait_recv()
    for p in other_chips:
        pre_copy(p, p).wait_recv()

    @pl.loop(0, width // tile)
    def _(i):
        at = pl.ds(pl.multiple_of(i * tile, tile), tile)
        grad_gated = part_buf[:, at] + sib_in[chip, :, at].astype(jnp.float32)
        for p in other_chips:
            grad_gated = grad_gated + pre_in[p, :, at].astype(jnp.float32)
        gc_buf[:, at] = (grad_gated * q_ref[:, at].astype(jnp.float32)).astype(jnp.bfloat16)
        gq_ref[:, at] = (grad_gated * conv_buf[:, at]).astype(jnp.bfloat16)

    gc_copy = remote(gc_buf, gcn_buf, gc_send, gc_recv, tok=lax.rem(tok + n_tok - 1, n_tok))

    @pl.when(has_previous)
    def _():
        gc_copy.start()

    @pl.loop(0, width // tile)
    def _(i):
        at = pl.ds(pl.multiple_of(i * tile, tile), tile)
        which = pl.ds(pl.multiple_of(i * tile_groups, tile_groups), tile_groups)
        extended = jnp.concatenate([rim_buf[:, at], kv_buf[:, at]], axis=0)
        local_buf[which, :] = filter_tile(extended, gc_buf[:, at], tile_groups, group_size)

    def owned(t):
        return pl.ds(pl.multiple_of(t * rows, rows), rows)

    def term_copy(t, slot):
        return remote(local_buf.at[owned(lax.rem(t, owners))], terms_buf.at[slot], term_send.at[t], term_recv.at[slot], tok=t)

    def sum_copy(t, owner):
        return remote(all_buf.at[owned(owner)], all_buf.at[owned(owner)], sum_send.at[t], sum_recv.at[owner], tok=t)

    def if_owner(t, action):
        if owners == n_tok:
            action()
        else:
            pl.when(t < owners)(action)

    for t in other_toks:
        if_owner(t, lambda t=t: term_copy(t, tok).start())

    def project(block, start, depth, first):
        @pl.loop(0, width // chunk)
        def _(j):
            at = pl.ds(pl.multiple_of(j * chunk, chunk), chunk)
            deep = pl.ds(pl.multiple_of(block * width + start, depth), depth)
            product = jnp.dot(
                gather[block, :, pl.ds(start, depth)], w_buf[deep, at], preferred_element_type=jnp.float32
            )
            total[:, at] = product if first else total[:, at] + product

    project(me, 0, width, True)
    for h in range(halves):
        own_copy(h, sibling).wait_recv()

    def sum_terms():
        for t in other_toks:
            term_copy(t, t).wait_recv()
        terms_buf[tok] = local_buf[owned(tok), :]
        all_buf[owned(tok), :] = jnp.sum(terms_buf[...], axis=0)
        for t in other_toks:
            sum_copy(t, tok).start()

    for h in range(halves):
        for p in other_chips:
            peer_copy(p, h, p * 2 + core, p).wait_recv()
            fwd_copy(p, h, p * 2 + core).start()
    project(sibling, 0, width, False)
    for p in other_chips:
        project(p * 2 + core, 0, width, False)
    if_owner(tok, sum_terms)
    for p in other_chips:
        for h in range(halves):
            fwd_copy(p, h, p * 2 + 1 - core).wait_recv()
        project(p * 2 + 1 - core, 0, width, False)
    out_ref[...] = total[...].astype(jnp.bfloat16)

    @pl.when(has_next)
    def _():
        gc_copy.wait_recv()

    @pl.when(jnp.logical_not(has_next))
    def _():
        gcn_buf[...] = jnp.zeros_like(gcn_buf)

    @pl.loop(0, width // tile)
    def _(i):
        at = pl.ds(pl.multiple_of(i * tile, tile), tile)
        which = pl.ds(pl.multiple_of(i * tile_groups, tile_groups), tile_groups)
        grads = jnp.concatenate([gc_buf[:, at], gcn_buf[:, at]], axis=0)
        grad_kv = backward_tile(f_ref[which, :], grads, group_size)
        gk_ref[:, at] = (grad_kv * v_ref[:, at].astype(jnp.float32)).astype(jnp.bfloat16)
        gv_ref[:, at] = (grad_kv * k_ref[:, at].astype(jnp.float32)).astype(jnp.bfloat16)

    for t in other_toks:
        if_owner(t, lambda t=t: sum_copy(t, t).wait_recv())
    gf_ref[...] = all_buf[...] * (1.0 / math.sqrt(length * n_tok * group_size))

    pl.when(has_next)(lambda: kv_copy.wait_send())
    pl.when(has_previous)(lambda: gc_copy.wait_send())
    for p in other_chips + [chip]:
        sib_copy(p).wait_send()
    for p in other_chips:
        pre_copy(p, chip).wait_send()
    for h in range(halves):
        own_copy(h, me).wait_send()
        for p in other_chips:
            peer_copy(p, h, me, chip).wait_send()
            fwd_copy(p, h, p * 2 + core).wait_send()
    for t in other_toks:
        if_owner(t, lambda t=t: term_copy(t, tok).wait_send())

    def sums_sent():
        for t in other_toks:
            sum_copy(t, tok).wait_send()

    if_owner(tok, sums_sent)


def local(queries, key_branch, value_branch, filters, out_weight, cotangent):
    length, width = queries.shape
    groups, kernel_size = filters.shape
    n_tok, n_wid = lax.axis_size("tok"), lax.axis_size("wid")
    chips = n_wid // 2
    tile, chunk = min(256, width), min(512, width)
    halves = 2 if width // tile % 2 == 0 else 1
    owners = min(n_tok, groups // 8)
    bf16, f32 = jnp.bfloat16, jnp.float32
    wide = jax.ShapeDtypeStruct((length, width), bf16)
    dma = pltpu.SemaphoreType.DMA
    vmem = pl.BlockSpec(memory_space=pltpu.VMEM)
    return pl.pallas_call(
        functools.partial(kernel, (n_tok, n_wid, tile, chunk, halves, owners)),
        in_specs=[vmem] * 4 + [pl.BlockSpec(memory_space=pl.ANY), vmem],
        out_specs=[vmem] * 5,
        out_shape=[wide] * 4 + [jax.ShapeDtypeStruct(filters.shape, f32)],
        scratch_shapes=[
            pltpu.VMEM(out_weight.shape, bf16),
            pltpu.VMEM((length, width), bf16),
            pltpu.VMEM((length, width), bf16),
            pltpu.VMEM((length, width), f32),
            pltpu.VMEM((length, width), f32),
            pltpu.VMEM((chips, length, width), bf16),
            pltpu.VMEM((chips, length, width), bf16),
            pltpu.VMEM((chips, length, width), bf16),
            pltpu.VMEM((chips, length, width), bf16),
            pltpu.VMEM((n_wid, length, width), bf16),
            pltpu.VMEM((length, width), f32),
            pltpu.VMEM((length, width), bf16),
            pltpu.VMEM((length, width), bf16),
            pltpu.VMEM(filters.shape, f32),
            pltpu.VMEM(filters.shape, f32),
            pltpu.VMEM((n_tok, groups // owners, kernel_size), f32),
            pltpu.VMEM(filters.shape, f32),
            dma((n_wid * (width // chunk),)),
            dma, dma,
            dma((chips,)), dma((chips,)), dma((chips,)), dma((chips,)),
            dma((halves,)), dma((halves,)),
            dma((chips * halves,)), dma((chips * halves,)), dma((chips * halves,)), dma((chips * halves,)),
            dma, dma,
            dma((n_tok,)), dma((n_tok,)), dma((n_tok,)), dma((n_tok,)),
        ],
        compiler_params=pltpu.CompilerParams(
            collective_id=0, has_side_effects=True, vmem_limit_bytes=60 * 2**20
        ),
        cost_estimate=pl.CostEstimate(
            flops=4 * length * width * width * n_wid, bytes_accessed=2 * width * width * n_wid, transcendentals=0
        ),
    )(queries, key_branch, value_branch, filters, out_weight, cotangent)


def solution(mesh):
    return jax.shard_map(
        local,
        mesh=mesh,
        in_specs=(
            P("tok", "wid"),
            P("tok", "wid"),
            P("tok", "wid"),
            P("wid", None),
            P(None, "wid"),
            P("tok", "wid"),
        ),
        out_specs=(
            P("tok", "wid"),
            P("tok", "wid"),
            P("tok", "wid"),
            P("tok", "wid"),
            P("wid", None),
        ),
        check_vma=False,
    )
```

time: 174 us -> 60.6 us (0.35)
  waiting for transfers between devices: 86.3 us -> 0 us
  matrix products: 39.5 us -> 0 us
  Pallas kernels: 19.2 us -> 50.5 us
  between operations: 13.9 us -> 0.64 us
  starting transfers between devices: 6.48 us -> 0 us
  local copies, waits for them, and re-layouts: 2.73 us -> 8.99 us
  other arithmetic: 4.78 us -> 0 us
    psum x1 -> x0, waiting for transfers between devices: 52.1 us -> none  [local(): grad_filters = lax.psum(local_terms, 'tok') * scale_factor]
    dot_general x2 -> x0, matrix products: 39.5 us -> none  [the longest x1 23 us: local(): lax.dot_general(out_weight, cotangent, (((1,), (1,)), ((), ())), preferre...]
    pallas_call x2 -> x1, Pallas kernels: 19.2 us -> 50.5 us  [local(): pl.pallas_call(functools.partial(kernel, (n_tok, n_wid, tile, chunk, halv...]
    ppermute x2 -> x0, waiting for transfers between devices: 24.3 us -> none  [shifted(): return lax.ppermute(block, axis, route)]
    reduce_scatter x1 -> x0, waiting for transfers between devices: 9.85 us -> none  [local(): lax.psum_scatter(partial, 'wid', scatter_dimension=0, tiled=True)]
    unnamed x18 -> x5, local copies, waits for them, and re-layouts: 2.58 us -> 8.99 us
    ppermute x2 -> x0, starting transfers between devices: 6.36 us -> none  [shifted(): return lax.ppermute(block, axis, route)]
    convert_element_type x2 -> x0, other arithmetic: 2.57 us -> none  [the longest x1 2.44 us: local(): grad_conv = (grad_gated * queries.astype(jnp.float32)).astype(jnp.bfloat16)]
  transfers between devices with their start and end apart: 5 -> 0, of which waited for: 4 -> 0; matrix products, arithmetic and copies ran while one was open for 12% -> 0% of each run, Pallas kernels for 11% -> 0%
where the time goes in v2:
time: 60.6 us; the launch traced here: 60.2 us
  Pallas kernels  50.5 us (83%)
  local copies, waits for them, and re-layouts  8.99 us (15%)
  between operations  0.64 us (1%)
    pallas_call x1, Pallas kernels, local(): pl.pallas_call(functools.partial(kernel, (n_tok, n_wid, tile, chunk, halv...  50.5 us
    unnamed x5, local copies, waits for them, and re-layouts  8.99 us

profile of v2, /device:TPU:0, one launch (start us, length us, event | category | flops | bytes accessed | tf_op | source)
XLA Modules:
  0.0 60.2 jit_solution(9392290755902236013)
XLA Ops:
  0.6 50.5 %shard_map.101 = (bf16[128,2048]{1,0:T(8,128)(2,1)}, bf16[128,2048]{1,0:T(8,128)(2,1)}, bf16[128,2048]{1,0:T(8,128)(2,1)}, bf16[128,2048]{1,0:T(8,128)(2,1)}, f32[128,128]{1,0:T(8,128)}) custom-call(bf16[128,2048]{1,0:T(8,128)(2,1)} %q_ref.1, bf16[128,2048]{1,0:T(8,128)(2,1)} %k_ref.1, bf16[128,2048]{1,0:T(8,128)(2,1)} %v_ref.1, f32[128,128]{1,0:T(8,128)} %f_ref.1, ...), custom_call_target="tpu_custom_call" | custom-call | flops 8589934592 | bytes 33554432 | tf_op jit(solution)/shard_map/pallas_call | solution.py:348
  51.2 1.9 %copy.16 = bf16[128,2048]{1,0:T(8,128)(2,1)} copy(bf16[128,2048]{1,0:T(8,128)(2,1)} %get-tuple-element.10) | data formatting | bytes 1048576
  53.1 1.9 %copy.17 = bf16[128,2048]{1,0:T(8,128)(2,1)} copy(bf16[128,2048]{1,0:T(8,128)(2,1)} %get-tuple-element.11) | data formatting | bytes 1048576
  54.9 1.9 %copy.18 = bf16[128,2048]{1,0:T(8,128)(2,1)} copy(bf16[128,2048]{1,0:T(8,128)(2,1)} %get-tuple-element.12) | data formatting | bytes 1048576
  56.8 1.9 %copy.19 = bf16[128,2048]{1,0:T(8,128)(2,1)} copy(bf16[128,2048]{1,0:T(8,128)(2,1)} %get-tuple-element.13) | data formatting | bytes 1048576
  58.7 1.5 %copy.20 = f32[128,128]{1,0:T(8,128)} copy(f32[128,128]{1,0:T(8,128)} %get-tuple-element.14) | data formatting | bytes 131072

commit v3 on v2

--- a/solution.py
+++ b/solution.py
@@ -17,64 +17,53 @@
     return pltpu.roll(jnp.broadcast_to(row, (kernel, kernel)), 0, 1, stride=1, stride_axis=0)
 
 
-def forward_tile(filters_rev, extended, group_size):
-    groups, kernel = filters_rev.shape
-    tile = extended.shape[1]
-    row, lane = iota((kernel, kernel), 0), iota((kernel, kernel), 1)
-    now = lane <= row
+def as_mask(condition):
+    return jnp.where(condition, 1.0, 0.0).astype(jnp.bfloat16)
+
+
+def conv_tile(filters, data, now, group_size, now_first):
+    groups, kernel = filters.shape
+    tile = data.shape[1]
+    inside, outside = as_mask(now), as_mask(jnp.logical_not(now))
     owner = iota((kernel, tile), 1) // group_size
     result = jnp.zeros((kernel, tile), jnp.float32)
     for g in range(groups):
-        ring = circulant(filters_rev[g : g + 1], kernel)
-        both = jnp.concatenate(
-            [jnp.where(now, 0.0, ring).astype(jnp.bfloat16), jnp.where(now, ring, 0.0).astype(jnp.bfloat16)],
-            axis=1,
-        )
-        part = jnp.dot(both, extended, preferred_element_type=jnp.float32)
+        ring = circulant(filters[g : g + 1], kernel).astype(jnp.bfloat16)
+        pair = [ring * inside, ring * outside] if now_first else [ring * outside, ring * inside]
+        part = jnp.dot(jnp.concatenate(pair, axis=1), data, preferred_element_type=jnp.float32)
         result = jnp.where(owner == g, part, result)
     return result
 
 
+def forward_tile(filters_rev, extended, group_size):
+    kernel = filters_rev.shape[1]
+    now = iota((kernel, kernel), 1) <= iota((kernel, kernel), 0)
+    return conv_tile(filters_rev, extended, now, group_size, False)
+
+
 def backward_tile(filters, grads, group_size):
-    groups, kernel = filters.shape
-    tile = grads.shape[1]
-    row, lane = iota((kernel, kernel), 0), iota((kernel, kernel), 1)
-    now = row <= lane
-    owner = iota((kernel, tile), 1) // group_size
-    result = jnp.zeros((kernel, tile), jnp.float32)
-    for g in range(groups):
-        ring = circulant(filters[g : g + 1], kernel)
-        both = jnp.concatenate(
-            [jnp.where(now, ring, 0.0).astype(jnp.bfloat16), jnp.where(now, 0.0, ring).astype(jnp.bfloat16)],
-            axis=1,
-        )
-        part = jnp.dot(both, grads, preferred_element_type=jnp.float32)
-        result = jnp.where(owner == g, part, result)
-    return result
+    kernel = filters.shape[1]
+    now = iota((kernel, kernel), 0) <= iota((kernel, kernel), 1)
+    return conv_tile(filters, grads, now, group_size, True)
 
 
 def filter_tile(extended, own_grads, groups, group_size):
     kernel, tile = own_grads.shape
     row, lane = iota((kernel, kernel), 0), iota((kernel, kernel), 1)
-    now = row + lane >= kernel - 1
-    owner = iota((2 * kernel, tile), 1) // group_size
-    mirror = jnp.where(row + lane == kernel - 1, 1.0, 0.0).astype(jnp.bfloat16)
-    extended = jnp.concatenate(
-        [
-            jnp.dot(mirror, half, preferred_element_type=jnp.float32).astype(jnp.bfloat16)
-            for half in (extended[:kernel], extended[kernel:])
-        ],
-        axis=0,
-    )
+    now = row + lane <= kernel - 1
+    owner = iota((kernel, tile), 1) // group_size
+    mirrored = jnp.dot(
+        as_mask(row + lane == kernel - 1), own_grads, preferred_element_type=jnp.float32
+    ).astype(jnp.bfloat16)
     rows = []
     for g in range(groups):
         part = lax.dot_general(
-            jnp.where(owner == g, extended, jnp.zeros_like(extended)),
-            own_grads,
+            mirrored * as_mask(owner == g),
+            extended,
             (((1,), (1,)), ((), ())),
             preferred_element_type=jnp.float32,
         )
-        square = jnp.where(now, part[kernel:], part[:kernel])
+        square = jnp.where(now, part[:, kernel:], part[:, :kernel])
         aligned = pltpu.roll(square, 1, 1, stride=1, stride_axis=0)
         rows.append(jnp.sum(aligned, axis=0, keepdims=True))
     return jnp.concatenate(rows, axis=0)
@@ -83,7 +72,7 @@
 def kernel(
     sizes,
     q_ref, k_ref, v_ref, f_ref, w_ref, cot_ref,
-    out_ref, gq_ref, gk_ref, gv_ref, gf_ref,
+    out_ref, gq_ref, own_out, next_out, gf_ref,
     w_buf, kv_buf, rim_buf, conv_buf, part_buf, sib_out, sib_in, pre_out, pre_in,
     gather, total, gc_buf, gcn_buf, frev_buf, local_buf, terms_buf, all_buf,
     w_sem, kv_send, kv_recv, sib_send, sib_recv, pre_send, pre_recv,
@@ -95,10 +84,10 @@
     groups, kernel_size = f_ref.shape
     group_size = width // groups
     tile_groups = tile // group_size
-    per_block = width // chunk
+    half = width // halves
+    per_piece = half // chunk
     chips = n_wid // 2
     rows = groups // owners
-    half = width // halves
     tok, me = lax.axis_index("tok"), lax.axis_index("wid")
     chip, core = me // 2, lax.rem(me, 2)
     sibling = chip * 2 + 1 - core
@@ -106,14 +95,16 @@
     other_toks = [lax.rem(tok + off, n_tok) for off in range(1, n_tok)]
     order = []
     for p in other_chips + [chip]:
-        order += [p * 2 + 1 - core, p * 2 + core]
+        for h in range(halves):
+            order += [(p, p * 2 + 1 - core, h), (p, p * 2 + core, h)]
 
     def w_copy(position, j):
-        at = pl.ds(pl.multiple_of(order[position] * width + j * chunk, chunk), chunk)
-        return pltpu.make_async_copy(w_ref.at[at], w_buf.at[at], w_sem.at[position * per_block + j])
-
-    for position in range(n_wid):
-        for j in range(per_block):
+        start = order[position][1] * width + order[position][2] * half + j * chunk
+        at = pl.ds(pl.multiple_of(start, chunk), chunk)
+        return pltpu.make_async_copy(w_ref.at[at], w_buf.at[at], w_sem.at[position * per_piece + j])
+
+    for position in range(len(order)):
+        for j in range(per_piece):
             w_copy(position, j).start()
 
     def remote(src, dst, send, recv, **where):
@@ -139,31 +130,43 @@
 
     cot = cot_ref[...]
 
-    def sib_copy(p):
-        return remote(sib_out.at[p], sib_in.at[p], sib_send.at[p], sib_recv.at[p], wid=sibling)
-
-    def pre_copy(p, slot):
-        return remote(pre_out.at[p], pre_in.at[slot], pre_send.at[p], pre_recv.at[slot], wid=p * 2 + core)
-
-    for position in range(n_wid):
-        block = order[position]
-
-        @pl.loop(0, per_block)
+    def sib_copy(p, h):
+        at, sem = pl.ds(h * half, half), p * halves + h
+        return remote(sib_out.at[p, :, at], sib_in.at[p, :, at], sib_send.at[sem], sib_recv.at[sem], wid=sibling)
+
+    def pre_copy(p, slot, h):
+        at = pl.ds(h * half, half)
+        return remote(
+            pre_out.at[p, :, at], pre_in.at[slot, :, at],
+            pre_send.at[p * halves + h], pre_recv.at[slot * halves + h], wid=p * 2 + core,
+        )
+
+    def send_sum(p, h):
+        at = pl.ds(h * half, half)
+        sib_copy(p, h).wait_recv()
+        pre_out[p, :, at] = (part_buf[:, at] + sib_in[p, :, at].astype(jnp.float32)).astype(jnp.bfloat16)
+        pre_copy(p, chip, h).start()
+
+    waiting = None
+    for position, (p, block, h) in enumerate(order):
+
+        @pl.loop(0, per_piece)
         def _(j):
             w_copy(position, j).wait()
-            at = pl.ds(pl.multiple_of(block * width + j * chunk, chunk), chunk)
-            part_buf[:, pl.ds(pl.multiple_of(j * chunk, chunk), chunk)] = lax.dot_general(
+            at = pl.ds(pl.multiple_of(block * width + h * half + j * chunk, chunk), chunk)
+            part_buf[:, pl.ds(pl.multiple_of(h * half + j * chunk, chunk), chunk)] = lax.dot_general(
                 cot, w_buf[at, :], (((1,), (1,)), ((), ())), preferred_element_type=jnp.float32
             )
 
-        p = (other_chips + [chip])[position // 2]
         if position % 2 == 0:
-            sib_out[p] = part_buf[...].astype(jnp.bfloat16)
-            sib_copy(p).start()
-        elif position < n_wid - 1:
-            sib_copy(p).wait_recv()
-            pre_out[p] = (part_buf[...] + sib_in[p].astype(jnp.float32)).astype(jnp.bfloat16)
-            pre_copy(p, chip).start()
+            at = pl.ds(h * half, half)
+            sib_out[p, :, at] = part_buf[:, at].astype(jnp.bfloat16)
+            sib_copy(p, h).start()
+            if waiting is not None:
+                send_sum(*waiting)
+                waiting = None
+        elif position < 2 * halves * (chips - 1):
+            waiting = (p, h)
 
     flip = jnp.where(
         lax.rem(iota((kernel_size, kernel_size), 0) + iota((kernel_size, kernel_size), 1), kernel_size) == 0, 1.0, 0.0
@@ -211,9 +214,10 @@
             peer_copy(p, h, me, chip).start()
         own_copy(h, me).start()
 
-    sib_copy(chip).wait_recv()
-    for p in other_chips:
-        pre_copy(p, p).wait_recv()
+    for h in range(halves):
+        sib_copy(chip, h).wait_recv()
+        for p in other_chips:
+            pre_copy(p, p, h).wait_recv()
 
     @pl.loop(0, width // tile)
     def _(i):
@@ -236,6 +240,10 @@
         which = pl.ds(pl.multiple_of(i * tile_groups, tile_groups), tile_groups)
         extended = jnp.concatenate([rim_buf[:, at], kv_buf[:, at]], axis=0)
         local_buf[which, :] = filter_tile(extended, gc_buf[:, at], tile_groups, group_size)
+
+    local_buf[...] = jnp.dot(
+        local_buf[...], flip.astype(jnp.float32), preferred_element_type=jnp.float32, precision=lax.Precision.HIGHEST
+    )
 
     def owned(t):
         return pl.ds(pl.multiple_of(t * rows, rows), rows)
@@ -299,25 +307,19 @@
     def _():
         gcn_buf[...] = jnp.zeros_like(gcn_buf)
 
-    @pl.loop(0, width // tile)
-    def _(i):
-        at = pl.ds(pl.multiple_of(i * tile, tile), tile)
-        which = pl.ds(pl.multiple_of(i * tile_groups, tile_groups), tile_groups)
-        grads = jnp.concatenate([gc_buf[:, at], gcn_buf[:, at]], axis=0)
-        grad_kv = backward_tile(f_ref[which, :], grads, group_size)
-        gk_ref[:, at] = (grad_kv * v_ref[:, at].astype(jnp.float32)).astype(jnp.bfloat16)
-        gv_ref[:, at] = (grad_kv * k_ref[:, at].astype(jnp.float32)).astype(jnp.bfloat16)
-
+    own_out[...] = gc_buf[...]
+    next_out[...] = gcn_buf[...]
     for t in other_toks:
         if_owner(t, lambda t=t: sum_copy(t, t).wait_recv())
-    gf_ref[...] = all_buf[...] * (1.0 / math.sqrt(length * n_tok * group_size))
+    gf_ref[...] = all_buf[...]
 
     pl.when(has_next)(lambda: kv_copy.wait_send())
     pl.when(has_previous)(lambda: gc_copy.wait_send())
-    for p in other_chips + [chip]:
-        sib_copy(p).wait_send()
-    for p in other_chips:
-        pre_copy(p, chip).wait_send()
+    for h in range(halves):
+        for p in other_chips + [chip]:
+            sib_copy(p, h).wait_send()
+        for p in other_chips:
+            pre_copy(p, chip, h).wait_send()
     for h in range(halves):
         own_copy(h, me).wait_send()
         for p in other_chips:
@@ -331,6 +333,25 @@
             sum_copy(t, tok).wait_send()
 
     if_owner(tok, sums_sent)
+
+
+def last_kernel(
+    group_size, tile, scale, out_ref, gq_ref, own_ref, next_ref, sums_ref, k_ref, v_ref, f_ref,
+    out, gq, gk, gv, gf,
+):
+    out[...] = out_ref[...]
+    gq[...] = gq_ref[...]
+    gf[...] = sums_ref[...] * scale
+    tile_groups = tile // group_size
+
+    @pl.loop(0, k_ref.shape[1] // tile)
+    def _(i):
+        at = pl.ds(pl.multiple_of(i * tile, tile), tile)
+        which = pl.ds(pl.multiple_of(i * tile_groups, tile_groups), tile_groups)
+        grads = jnp.concatenate([own_ref[:, at], next_ref[:, at]], axis=0)
+        grad_kv = backward_tile(f_ref[which, :], grads, group_size)
+        gk[:, at] = (grad_kv * v_ref[:, at].astype(jnp.float32)).astype(jnp.bfloat16)
+        gv[:, at] = (grad_kv * k_ref[:, at].astype(jnp.float32)).astype(jnp.bfloat16)
 
 
 def local(queries, key_branch, value_branch, filters, out_weight, cotangent):
@@ -338,14 +359,16 @@
     groups, kernel_size = filters.shape
     n_tok, n_wid = lax.axis_size("tok"), lax.axis_size("wid")
     chips = n_wid // 2
-    tile, chunk = min(256, width), min(512, width)
-    halves = 2 if width // tile % 2 == 0 else 1
+    group_size = width // groups
+    tile, halves = min(128, width // 2), 2
+    chunk = min(512, width // halves)
+    step = min(512, width)
     owners = min(n_tok, groups // 8)
     bf16, f32 = jnp.bfloat16, jnp.float32
     wide = jax.ShapeDtypeStruct((length, width), bf16)
     dma = pltpu.SemaphoreType.DMA
     vmem = pl.BlockSpec(memory_space=pltpu.VMEM)
-    return pl.pallas_call(
+    results = pl.pallas_call(
         functools.partial(kernel, (n_tok, n_wid, tile, chunk, halves, owners)),
         in_specs=[vmem] * 4 + [pl.BlockSpec(memory_space=pl.ANY), vmem],
         out_specs=[vmem] * 5,
@@ -370,7 +393,7 @@
             pltpu.VMEM(filters.shape, f32),
             dma((n_wid * (width // chunk),)),
             dma, dma,
-            dma((chips,)), dma((chips,)), dma((chips,)), dma((chips,)),
+            dma((chips * halves,)), dma((chips * halves,)), dma((chips * halves,)), dma((chips * halves,)),
             dma((halves,)), dma((halves,)),
             dma((chips * halves,)), dma((chips * halves,)), dma((chips * halves,)), dma((chips * halves,)),
             dma, dma,
@@ -383,6 +406,16 @@
             flops=4 * length * width * width * n_wid, bytes_accessed=2 * width * width * n_wid, transcendentals=0
         ),
     )(queries, key_branch, value_branch, filters, out_weight, cotangent)
+    channels = pl.BlockSpec((length, step), lambda i: (0, i))
+    by_group = pl.BlockSpec((step // group_size, kernel_size), lambda i: (i, 0))
+    scale = 1.0 / math.sqrt(length * n_tok * group_size)
+    return pl.pallas_call(
+        functools.partial(last_kernel, group_size, tile, scale),
+        grid=(width // step,),
+        in_specs=[channels] * 4 + [by_group, channels, channels, by_group],
+        out_specs=[channels] * 4 + [by_group],
+        out_shape=[wide] * 4 + [jax.ShapeDtypeStruct(filters.shape, f32)],
+    )(*results, key_branch, value_branch, filters)
 
 
 def solution(mesh):

time: 60.6 us -> 55.6 us (0.917)
  local copies, waits for them, and re-layouts: 8.99 us -> 0 us
  Pallas kernels: 50.5 us -> 54.8 us
    unnamed x5 -> x0, local copies, waits for them, and re-layouts: 8.99 us -> none
    pallas_call x0 -> x1, Pallas kernels: none -> 7.94 us  [local(): pl.pallas_call(functools.partial(last_kernel, group_size, tile, scale), g...]
    pallas_call x1, Pallas kernels: 50.5 us -> 46.8 us  [local(): pl.pallas_call(functools.partial(kernel, (n_tok, n_wid, tile, chunk, halv...]
where the time goes in v3:
time: 55.6 us; the launch traced here: 55.4 us
  Pallas kernels  54.8 us (99%)
  between operations  0.64 us (1%)
    pallas_call x1, Pallas kernels, local(): pl.pallas_call(functools.partial(kernel, (n_tok, n_wid, tile, chunk, halv...  46.8 us
    pallas_call x1, Pallas kernels, local(): pl.pallas_call(functools.partial(last_kernel, group_size, tile, scale), g...  7.94 us

profile of v3, /device:TPU:0, one launch (start us, length us, event | category | flops | bytes accessed | tf_op | source)
XLA Modules:
  0.0 55.4 jit_solution(11057502185539589077)
XLA Ops:
  0.6 46.8 %shard_map.101 = (bf16[128,2048]{1,0:T(8,128)(2,1)}, bf16[128,2048]{1,0:T(8,128)(2,1)}, bf16[128,2048]{1,0:T(8,128)(2,1)}, bf16[128,2048]{1,0:T(8,128)(2,1)}, f32[128,128]{1,0:T(8,128)}) custom-call(bf16[128,2048]{1,0:T(8,128)(2,1)} %q_ref.1, bf16[128,2048]{1,0:T(8,128)(2,1)} %k_ref.3, bf16[128,2048]{1,0:T(8,128)(2,1)} %v_ref.3, f32[128,128]{1,0:T(8,128)} %f_ref.3, ...), custom_call_target="tpu_custom_call" | custom-call | flops 8589934592 | bytes 33554432 | tf_op jit(solution)/shard_map/pallas_call | solution.py:371
  47.5 7.9 %shard_map.102 = (bf16[128,2048]{1,0:T(8,128)(2,1)}, bf16[128,2048]{1,0:T(8,128)(2,1)}, bf16[128,2048]{1,0:T(8,128)(2,1)}, bf16[128,2048]{1,0:T(8,128)(2,1)}, f32[128,128]{1,0:T(8,128)}) custom-call(bf16[128,2048]{1,0:T(8,128)(2,1)} %get-tuple-element.10.out_ref, bf16[128,2048]{1,0:T(8,128)(2,1)} %get-tuple-element.11.gq_ref, ...), custom_call_target="tpu_custom_call" | custom-call | tf_op jit(solution)/shard_map/pallas_call | solution.py:412

commit v4 on v3

--- a/solution.py
+++ b/solution.py
@@ -360,7 +360,7 @@
     n_tok, n_wid = lax.axis_size("tok"), lax.axis_size("wid")
     chips = n_wid // 2
     group_size = width // groups
-    tile, halves = min(128, width // 2), 2
+    tile, halves = min(128, width // 2), min(4, max(2, width // 128))
     chunk = min(512, width // halves)
     step = min(512, width)
     owners = min(n_tok, groups // 8)

time: 55.6 us -> 55.9 us (level)
  no operation moved by 1% of the time
where the time goes in v4:
time: 55.9 us; the launch traced here: 55.7 us
  Pallas kernels  55.1 us (99%)
  between operations  0.64 us (1%)
    pallas_call x1, Pallas kernels, local(): pl.pallas_call(functools.partial(kernel, (n_tok, n_wid, tile, chunk, halv...  47.1 us
    pallas_call x1, Pallas kernels, local(): pl.pallas_call(functools.partial(last_kernel, group_size, tile, scale), g...  7.94 us

profile of v4, /device:TPU:0, one launch (start us, length us, event | category | flops | bytes accessed | tf_op | source)
XLA Modules:
  0.0 55.7 jit_solution(8175573892757210637)
XLA Ops:
  0.6 47.1 %shard_map.101 = (bf16[128,2048]{1,0:T(8,128)(2,1)}, bf16[128,2048]{1,0:T(8,128)(2,1)}, bf16[128,2048]{1,0:T(8,128)(2,1)}, bf16[128,2048]{1,0:T(8,128)(2,1)}, f32[128,128]{1,0:T(8,128)}) custom-call(bf16[128,2048]{1,0:T(8,128)(2,1)} %q_ref.1, bf16[128,2048]{1,0:T(8,128)(2,1)} %k_ref.3, bf16[128,2048]{1,0:T(8,128)(2,1)} %v_ref.3, f32[128,128]{1,0:T(8,128)} %f_ref.3, ...), custom_call_target="tpu_custom_call" | custom-call | flops 8589934592 | bytes 33554432 | tf_op jit(solution)/shard_map/pallas_call | solution.py:371
  47.8 7.9 %shard_map.102 = (bf16[128,2048]{1,0:T(8,128)(2,1)}, bf16[128,2048]{1,0:T(8,128)(2,1)}, bf16[128,2048]{1,0:T(8,128)(2,1)}, bf16[128,2048]{1,0:T(8,128)(2,1)}, f32[128,128]{1,0:T(8,128)}) custom-call(bf16[128,2048]{1,0:T(8,128)(2,1)} %get-tuple-element.10.out_ref, bf16[128,2048]{1,0:T(8,128)(2,1)} %get-tuple-element.11.gq_ref, ...), custom_call_target="tpu_custom_call" | custom-call | tf_op jit(solution)/shard_map/pallas_call | solution.py:412
